TPU v7x, 512 devices: a whole 4x4x16 slice. The times are simulated.
512 devices in a mesh: dp: 8 (over x, core), mem: 64 (over z, y).
Axes of the slice: x: 4, y: 4, z: 16, core: 2. Of those that a mesh axis runs over, the one named last changes fastest.
Arguments:
- lookup_slot: int32 [65536, 4, 32], P(('dp', 'mem')), may hold values from 0 to 511
- lookup_weight: float32 [65536, 4, 32], P(('dp', 'mem')), may hold values from 0.02 to 0.3
- owner_route: int32 [65536, 2], P(('dp', 'mem')), may hold values from 0 to 63, all different within a row; in each aligned block of 128 rows (0 to 127, 128 to 255, ...) at most 8 rows name the same one
- values: bfloat16 [16384, 4096], P('mem'), may hold values from -1.5 to 1.5
- out_grad: bfloat16 [65536, 4096], P(('dp', 'mem')), may hold values from -0.3984375 to 0.3984375
Outputs:
- memory_out: bfloat16 [65536, 4096], P(('dp', 'mem'))
- grad_values: float32 [16384, 4096], P('mem', 'dp')
- grad_weight: float32 [65536, 4, 32], P(('dp', 'mem'))
Inputs may be any that keep to these rules, and one draw needn't show every extreme that they name: `owner_route`: each row names 2 different owners; among the rows of one device no owner is named more than 8 times, a bound that some block reaches.
All inputs are finite; a program needn't handle non-finite values.
Results may differ from a plain program's by a relative error of at most 0.006.
Values may be sent and summed in bfloat16 or wider, within the bound.
A program may use at most 64 MiB of HBM per device.

v0:
```python
import functools

import jax
import jax.numpy as jnp
from jax import lax
from jax.experimental import pallas as pl
from jax.experimental.pallas import tpu as pltpu
from jax.sharding import PartitionSpec as P

MESH = pl.DeviceIdType.MESH
X, K, Z, Y = 4, 2, 16, 4
C = X * K
TOK, PICKS, ROWS, FEAT, CAP = 128, 128, 256, 512, 8
HALF = ROWS // 2
SLOTS = Z * CAP
MSG = SLOTS + 16
F32, BF16 = jnp.float32, jnp.bfloat16
NT = (((1,), (1,)), ((), ()))
TN = (((0,), (0,)), ((), ()))


class Ids:
    def __init__(self):
        self.count = 0

    def take(self, number=1):
        first = self.count
        self.count += number
        return first


def exchange(
    slot_in, weight_in, route_in, og, values,
    out, gv, pair,
    va, oga, wm, wa, ps, dense_t, slot_t, weight_t, route, pair_v, gv_v, pm, wt, gt, pt, ip, ir, ic, ix, iy, isrc,
    outp, ytr, ytl, yfr, yfl, rz, sz, ssem, rsem, lsem,
):
    dp, mem = lax.axis_index("dp"), lax.axis_index("mem")
    x, k = dp // K, dp % K
    z, y = mem // Y, mem % Y
    ids = Ids()
    sent = []

    def dev(dx=0, dk=0, dz=0, dy=0):
        to_dp = ((x + dx) % X) * K + (k + dk) % K
        to_mem = ((z + dz) % Z) * Y + (y + dy) % Y
        return (to_dp, to_mem)

    def cof(dx, dk):
        return ((x + dx) % X) * K + (k + dk) % K

    def copy(src, dst, sem, to):
        return pltpu.make_async_remote_copy(
            src_ref=src, dst_ref=dst, send_sem=ssem.at[sem], recv_sem=rsem.at[sem],
            device_id=to, device_id_type=MESH,
        )

    def send(src, dst, sem, to):
        one = copy(src, dst, sem, to)
        one.start()
        sent.append(one)

    def arrived(dst, sem):
        copy(dst, dst, sem, dev(dk=1)).wait_recv()

    def cols(index):
        return pl.ds(pl.multiple_of(index * FEAT, FEAT), FEAT)

    c = dp
    own_v = [
        pltpu.make_async_copy(
            values.at[pl.ds(h * HALF, HALF), cols(c)], va.at[z, h], lsem.at[h]
        )
        for h in range(2)
    ]
    for one in own_v:
        one.start()
    own_og = pltpu.make_async_copy(og.at[:, cols(c)], oga.at[c, y], lsem.at[2])
    own_og.start()
    tables = [
        pltpu.make_async_copy(slot_in, slot_t, lsem.at[4]),
        pltpu.make_async_copy(weight_in, weight_t, lsem.at[5]),
        pltpu.make_async_copy(route_in, route, lsem.at[7]),
    ]
    for one in tables:
        one.start()

    barrier = pltpu.get_barrier_semaphore()
    others = [(dx, dk) for dx in range(X) for dk in range(K) if (dx, dk) != (0, 0)]
    partners = [dev(dz=1), dev(dz=Z - 1)] + [dev(dy=d) for d in range(1, Y)]
    partners += [dev(dx=dx, dk=dk) for dx, dk in others]
    for partner in partners:
        pl.semaphore_signal(barrier, inc=1, device_id=partner, device_id_type=MESH)
    pl.semaphore_wait(barrier, len(partners))

    hops = {("r", 0): 8, ("l", 0): 7, ("r", 1): 7, ("l", 1): 8}
    zid = {(key, s): ids.take() for key, n in hops.items() for s in range(1, n + 1)}

    def z_send(s, way, h):
        if s <= hops[way, h]:
            if way == "r":
                at, to = (z + Z - s + 1) % Z, dev(dz=1)
            else:
                at, to = (z + s - 1) % Z, dev(dz=Z - 1)
            block = values.at[pl.ds(h * HALF, HALF), cols(c)] if s == 1 else va.at[at, h]
            send(block, va.at[at, h], zid[((way, h), s)], to)

    def z_step(s, h):
        for way in ("r", "l"):
            if s <= hops[way, h]:
                at = (z + Z - s) % Z if way == "r" else (z + s) % Z
                arrived(va.at[at, h], zid[((way, h), s)])
                z_send(s + 1, way, h)

    order = [(0, 0), (0, 1), (1, 0), (1, 1), (3, 0), (3, 1), (2, 0), (2, 1)]
    cid = [ids.take() for _ in order]
    yr1 = [ids.take() for _ in order]
    yl1 = [ids.take() for _ in order]
    y2 = [ids.take() for _ in order]

    def c_send(i):
        dx, dk = order[i]
        to = cof(dx, dk)
        send(og.at[:, cols(to)], oga.at[c, y], cid[i], dev(dx=dx, dk=dk))

    def source(i):
        dx, dk = order[i]
        return cof(X - dx, dk)

    def y_send(i):
        held = oga.at[source(i), y]
        block = held if i else og.at[:, cols(c)]
        send(block, held, yr1[i], dev(dy=1))
        send(block, held, yl1[i], dev(dy=Y - 1))

    def c_step(i):
        arrived(oga.at[source(i), y], cid[i])
        y_send(i)

    def y_step(i):
        right = oga.at[source(i), (y + Y - 1) % Y]
        left = oga.at[source(i), (y + 1) % Y]
        if i % 2 == 0:
            arrived(right, yr1[i])
            send(right, right, y2[i], dev(dy=1))
            arrived(left, yl1[i])
        else:
            arrived(left, yl1[i])
            send(left, left, y2[i], dev(dy=Y - 1))
            arrived(right, yr1[i])

    def y_last(i):
        arrived(oga.at[source(i), (y + 2) % Y], y2[i])

    w1 = [ids.take() for _ in range(Y)]
    w2 = {(dx, dy): ids.take() for dx in range(X) for dy in range(Y)}
    w3 = {(dx, dy): ids.take() for dx in range(1, X) for dy in range(Y)}

    def w_piece(dy):
        at = (y + Y - dy) % Y
        if dy:
            arrived(wa.at[c, at], w1[dy])
        for dx in (1, 3, 2):
            send(wa.at[c, at], wa.at[c, at], w2[dx, dy], dev(dx=dx))
        send(wa.at[c, at], wa.at[c, at], w2[0, dy], dev(dk=1))

    def w_pass(dx, dy):
        block = wa.at[cof(X - dx, 0), (y + Y - dy) % Y]
        arrived(block, w2[dx, dy])
        send(block, block, w3[dx, dy], dev(dk=1))

    def w_last(dx):
        for dy in range(Y):
            block = wa.at[cof(X - dx, 1), (y + Y - dy) % Y]
            arrived(block, w3[dx, dy] if dx else w2[0, dy])

    for way, h in hops:
        z_send(1, way, h)
    for i in range(1, 8):
        c_send(i)
    y_send(0)
    c_step(1)

    def dense(a):
        columns = lax.broadcasted_iota(jnp.int32, (128, TOK), 0) + a * 128

        def spread(step, total):
            at = pl.multiple_of(step * 8, 8)
            slot_rows, weight_rows = slot_t[pl.ds(at, 8), :], weight_t[pl.ds(at, 8), :]
            for u in range(8):
                hit = columns == slot_rows[u : u + 1, :]
                total = total + jnp.where(hit, weight_rows[u : u + 1, :], 0.0)
            return total

        total = lax.fori_loop(0, PICKS // 8, spread, jnp.zeros((128, TOK), F32))
        dense_t[pl.ds(a * 128, 128), :] = total.astype(BF16)

    for one in tables:
        one.wait()
    dense(0)
    z_step(1, 0)
    dense(1)
    c_step(2)
    dense(2)
    z_step(1, 1)
    dense(3)

    lane = lax.broadcasted_iota(jnp.int32, (TOK, TOK), 1)
    row = lax.broadcasted_iota(jnp.int32, (TOK, TOK), 0)
    owner = [route[0:1, :], route[1:2, :]]
    number = lax.broadcasted_iota(jnp.int32, (Z * Y, TOK), 0)
    hits = [jnp.where(number == one, 1.0, 0.0) for one in owner]
    earlier = jnp.where(row < lane, 1.0, 0.0).astype(BF16)
    ranks = [jnp.dot(hit.astype(BF16), earlier, preferred_element_type=F32) for hit in hits]
    ranks[1] = ranks[1] + jnp.sum(hits[0], axis=1, keepdims=True)
    ranks = [
        jnp.sum(hit * rank, axis=0, keepdims=True).astype(jnp.int32)
        for hit, rank in zip(hits, ranks)
    ]

    slot_ids = lax.broadcasted_iota(jnp.int32, (SLOTS, TOK), 0)
    for to in range(Y):
        total = jnp.zeros((SLOTS, ROWS), F32)
        lanes = []
        for j in range(2):
            here, group = owner[j] % Y == to, owner[j] // Y
            place = jnp.where(here, group * CAP + ranks[j], -1)
            one = jnp.where(slot_ids == place, 1.0, 0.0).astype(BF16)
            ps[j, pl.ds(to * SLOTS, SLOTS), :] = one
            total = total + lax.dot_general(
                one, dense_t[pl.ds(j * ROWS, ROWS), :], NT, preferred_element_type=F32
            )
            spot = group * (2 * CAP) + ranks[j] + (y % 2) * CAP
            lanes.append(jnp.where(here, spot, -1).astype(F32))
        wm[to, pl.ds(0, SLOTS), :] = total.astype(BF16)
        wm[to, pl.ds(SLOTS, 16), :] = jnp.broadcast_to(
            jnp.concatenate(lanes, axis=1), (16, ROWS)
        ).astype(BF16)
    for dy in (1, 3, 2):
        send(wm.at[(y + dy) % Y], wa.at[c, y], w1[dy], dev(dy=dy))
    wa[c, y] = wm[y]
    w_piece(0)

    c_step(4)
    c_step(3)
    z_step(2, 0)
    c_step(5)
    y_step(0)
    y_step(1)
    z_step(2, 1)
    c_step(6)
    c_step(7)
    w_piece(1)
    w_piece(3)
    z_step(3, 0)
    w_piece(2)
    y_step(2)
    z_step(3, 1)
    y_step(4)
    w_pass(1, 0)
    w_pass(3, 0)
    w_pass(2, 0)
    z_step(4, 0)
    y_step(3)
    w_last(0)
    z_step(4, 1)
    y_step(5)

    def prepare(i):
        src = source(i)

        def half(yp, carry):
            pi = (src % K) * 8 + (src // K) * 2 + yp
            slots = lax.broadcasted_iota(jnp.int32, (ROWS, TOK), 0).astype(F32)
            at = pl.multiple_of(pi * 16, 16)
            parts = []
            for q in range(2):
                row = wa[src, yp * 2 + q, pl.ds(SLOTS, 16), :].astype(F32)[0:1, :]
                hit = jnp.where(slots == row[:, :TOK], 1.0, 0.0)
                hit = hit + jnp.where(slots == row[:, TOK:], 1.0, 0.0)
                pm[pi, :, pl.ds(q * TOK, TOK)] = hit.astype(BF16)
                part = wa[src, yp * 2 + q, pl.ds(0, SLOTS), :].astype(F32)
                parts.append(part.reshape(Z, CAP, ROWS))
            wt[:, pl.ds(at, 16), :] = jnp.concatenate(parts, axis=1).astype(BF16)
            return carry

        lax.fori_loop(0, 2, half, 0)

    def gather(i):
        src = source(i)

        def half(yp, carry):
            pi = (src % K) * 8 + (src // K) * 2 + yp
            at = pl.multiple_of(pi * 16, 16)
            tokens = oga[src, pl.ds(yp * 2, 2)].reshape(2 * TOK, FEAT)
            got = jnp.dot(pm[pi], tokens, preferred_element_type=F32)
            gt[:, pl.ds(at, 16), :] = got.astype(BF16).reshape(Z, 16, FEAT)
            return carry

        lax.fori_loop(0, 2, half, 0)

    def p_step(s):
        def side(u, carry):
            at = (z + Z + (1 - 2 * u) * s) % Z
            rows = va[at].reshape(ROWS, FEAT)
            pt[at] = jnp.dot(wt[at], rows, preferred_element_type=F32).astype(BF16)
            return carry

        lax.fori_loop(0, 1 if s in (0, 8) else 2, side, 0)

    rid = ids.take(32)

    def grad_part(at, h):
        rows = pl.ds(h * HALF, HALF)
        return lax.dot_general(wt[at, :, rows], gt[at], TN, preferred_element_type=F32)

    def r_step(s, h):
        def stream(way, carry):
            at = (z + Z + (1 - 2 * way) * (8 - s)) % Z
            total = grad_part(at, h)
            if s >= 2:
                arrived(rz.at[s - 1, way, h], rid + (s - 1) * 4 + way * 2 + h)
                total = total + rz[s - 1, way, h].astype(F32)
            sz[s, way, h] = total.astype(BF16)
            if s == 1:

                @pl.when(way == h)
                def _():
                    arrived(rz.at[0, way, h], rid + way * 2 + h)
                    more = total + rz[0, way, h].astype(F32)
                    sz[s, way, h] = more.astype(BF16)

            to_mem = ((z + Z + 1 - 2 * way) % Z) * Y + y
            copy(
                sz.at[s, way, h], rz.at[s, way, h], rid + s * 4 + way * 2 + h, (dp, to_mem)
            ).start()
            return carry

        if s == 0:
            stream(h, 0)
        else:
            lax.fori_loop(0, 2, stream, 0)

    def r_last(h):
        total = grad_part(z, h)
        for way in range(2):
            arrived(rz.at[7, way, h], rid + 28 + way * 2 + h)
            total = total + rz[7, way, h].astype(F32)
        gv_v[pl.ds(h * HALF, HALF), :] = total
        part = pl.ds(h * HALF, HALF)
        done = pltpu.make_async_copy(gv_v.at[part], gv.at[part], lsem.at[h])
        done.start()
        return done

    def r_drain(first, last):
        def drain(i, carry):
            block = sz.at[i // 4, (i // 2) % 2, i % 2]

            @pl.when((i != 1) & (i != 2))
            def _():
                copy(block, block, rid + i, dev(dz=1)).wait_send()

            return carry

        lax.fori_loop(first, last, drain, 0)

    i1 = ids.take()
    i2 = [ids.take() for _ in range(4)]
    i3 = [ids.take() for _ in range(4)]
    m1r = [ids.take() for _ in range(4)]
    m1l = [ids.take() for _ in range(4)]
    mr = [ids.take() for _ in range(8)]
    ml = [ids.take() for _ in range(8)]
    oid = [ids.take() for _ in order]
    far, up, down = (y + 2) % Y, (y + 1) % Y, (y + Y - 1) % Y
    couples = [(6, 7), (2, 3), (4, 5), (0, 1)]

    def to_of(i):
        dx, dk = order[i]
        return cof(dx, dk)

    def scatter(i):
        src = to_of(i)

        def half(yp, carry):
            pi = (src % K) * 8 + (src // K) * 2 + yp
            at = pl.multiple_of(pi * 16, 16)
            parts = pt[:, pl.ds(at, 16), :].reshape(ROWS, FEAT)
            got = lax.dot_general(pm[pi], parts, TN, preferred_element_type=F32)
            outp[src, pl.ds(yp * 2, 2)] = got.astype(BF16).reshape(2, TOK, FEAT)
            return carry

        lax.fori_loop(0, 2, half, 0)

    def m_first(n):
        e, o = couples[n]
        scatter(e)
        send(outp.at[to_of(e), far], ytr.at[n], m1r[n], dev(dy=1))
        send(outp.at[to_of(e), down], yfl.at[e], ml[e], dev(dy=Y - 1))
        scatter(o)
        send(outp.at[to_of(o), far], ytl.at[n], m1l[n], dev(dy=Y - 1))
        send(outp.at[to_of(o), up], yfr.at[o], mr[o], dev(dy=1))

    def m_second(n):
        e, o = couples[n]
        at = to_of(e)
        arrived(ytr.at[n], m1r[n])
        outp[at, up] = (outp[at, up].astype(F32) + ytr[n].astype(F32)).astype(BF16)
        send(outp.at[at, up], yfr.at[e], mr[e], dev(dy=1))
        at = to_of(o)
        arrived(ytl.at[n], m1l[n])
        outp[at, down] = (outp[at, down].astype(F32) + ytl[n].astype(F32)).astype(BF16)
        send(outp.at[at, down], yfl.at[o], ml[o], dev(dy=Y - 1))

    def m_final(n):
        for i in couples[n]:
            dx, dk = order[i]
            to = to_of(i)
            arrived(yfr.at[i], mr[i])
            arrived(yfl.at[i], ml[i])
            total = outp[to, y].astype(F32) + yfr[i].astype(F32) + yfl[i].astype(F32)
            outp[to, y] = total.astype(BF16)
            if i == 0:
                own = pltpu.make_async_copy(outp.at[to, y], out.at[:, cols(c)], lsem.at[3])
                own.start()
                own.wait()
            else:
                send(outp.at[to, y], out.at[:, cols(c)], oid[i], dev(dx=dx, dk=dk))

    def inner(at, carry):
        rows = va[at].reshape(ROWS, FEAT)
        got = lax.dot_general(gt[at], rows, NT, preferred_element_type=F32)
        ip[:, :, at] = got.astype(BF16).reshape(K, X, 32, ROWS)
        return carry

    def add_core(i, carry):
        xx = i // 4
        at = pl.ds((i % 4) * 4, 4)
        ic[xx, at] = (ip[k, xx, at].astype(F32) + ir[xx, at].astype(F32)).astype(BF16)
        return carry

    def add_chips(at, carry):
        total = ic[x, at].astype(F32)
        for i in range(3):
            total = total + ix[i, at].astype(F32)
        for q in range(4):
            iy[q, at] = total[q * CAP : (q + 1) * CAP, :]
        return carry

    for dy in (1, 3, 2):
        w_pass(1, dy)
        w_pass(3, dy)
    z_step(5, 0)
    for dy in (1, 3, 2):
        w_pass(2, dy)
    for one in own_v:
        one.wait()
    own_og.wait()
    prepare(0)
    prepare(1)
    y_step(6)
    y_step(7)
    z_step(5, 1)
    prepare(2)
    prepare(4)
    y_last(0)
    gather(0)
    y_last(1)
    gather(1)
    z_step(6, 0)
    prepare(6)
    w_last(1)
    w_last(3)
    prepare(3)
    prepare(5)
    y_last(2)
    gather(2)
    w_last(2)
    prepare(7)
    z_step(6, 1)
    for step in range(4):
        p_step(step)
    y_last(3)
    gather(3)
    y_last(4)
    gather(4)
    z_step(7, 0)
    p_step(4)
    p_step(5)
    y_last(5)
    gather(5)
    for i in (6, 7):
        y_last(i)
        gather(i)
    r_step(0, 0)
    z_step(7, 1)
    r_step(0, 1)
    p_step(6)
    z_step(8, 0)
    p_step(7)
    z_step(8, 1)
    p_step(8)
    early = len(sent)
    m_first(0)
    m_first(1)
    r_step(1, 0)
    r_step(1, 1)
    lax.fori_loop(0, Z // 2, inner, 0)
    r_step(2, 0)
    m_second(0)
    m_first(2)
    r_step(2, 1)
    lax.fori_loop(Z // 2, Z, inner, 0)
    send(ip.at[(k + 1) % K], ir, i1, dev(dk=1))
    r_step(3, 0)
    m_second(1)
    m_first(3)
    r_step(3, 1)
    arrived(ir, i1)
    lax.fori_loop(0, 16, add_core, 0)
    for dx in (1, 3, 2):
        send(ic.at[(x + dx) % X], ix.at[dx - 1], i2[dx], dev(dx=dx))
    r_step(4, 0)
    m_final(0)
    r_step(4, 1)
    m_second(2)
    r_step(5, 0)
    for one in sent[: early // 2]:
        one.wait_send()
    del sent[: early // 2]
    early -= early // 2
    r_step(5, 1)
    m_final(1)
    r_step(6, 0)
    m_second(3)
    for dx in (1, 3, 2):
        arrived(ix.at[dx - 1], i2[dx])
    lax.fori_loop(0, Z, add_chips, 0)
    for q in range(4):
        isrc[4, pl.ds(q * SLOTS, SLOTS), :] = iy[q].reshape(SLOTS, ROWS).astype(BF16)
    isrc[0, pl.ds(0, SLOTS), :] = isrc[4, pl.ds(pl.multiple_of(y * SLOTS, SLOTS), SLOTS), :]
    for i in range(1, 4):
        to = (y + i) % Y
        send(
            isrc.at[4, pl.ds(pl.multiple_of(to * SLOTS, SLOTS), SLOTS), :],
            isrc.at[i, pl.ds(0, SLOTS), :], i3[i], dev(dy=i),
        )
    r_step(6, 1)
    for one in sent[:early]:
        one.wait_send()
    del sent[:early]
    r_drain(0, 20)
    r_step(7, 0)
    m_final(2)
    r_step(7, 1)
    for i in range(1, 4):
        arrived(isrc.at[i, pl.ds(0, SLOTS), :], i3[i])
    for j in range(2):
        total = jnp.zeros((TOK, ROWS), F32)
        for i in range(4):
            at = pl.multiple_of(((y + Y - i) % Y) * SLOTS, SLOTS)
            total = total + lax.dot_general(
                ps[j, pl.ds(at, SLOTS), :], isrc[i, pl.ds(0, SLOTS), :], TN,
                preferred_element_type=F32,
            )
        pair_v[:, pl.ds(j * ROWS, ROWS)] = total
    pair_out = pltpu.make_async_copy(pair_v, pair, lsem.at[6])
    pair_out.start()
    m_final(3)
    gv_done = [r_last(0)]
    for i in range(1, 8):
        arrived(out.at[:, cols(source(i))], oid[i])
    gv_done.append(r_last(1))
    pair_out.wait()
    for one in sent:
        one.wait_send()
    r_drain(20, 32)
    for one in gv_done:
        one.wait()
    assert ids.count <= SEMS, ids.count


SEMS = 192


def pick(
    pair_in, slot_in, out_in, gv_in, out_ref, out_out, gv_out,
    pair_v, slot_v, picked, out_v, gv_v, fetch_sem, put_sem,
):
    number = 8
    blocks = [(pair_in, pair_v, None), (slot_in, slot_v, None)]
    for n in range(number):
        part = pl.ds(n * TOK // number, TOK // number)
        blocks.append((out_in.at[part], out_v.at[part], out_out.at[part]))
    for n in range(4):
        part = pl.ds(n * ROWS // 4, ROWS // 4)
        blocks.append((gv_in.at[part], gv_v.at[part], gv_out.at[part]))
    fetch = [
        pltpu.make_async_copy(src, held, fetch_sem.at[n])
        for n, (src, held, _) in enumerate(blocks)
    ]
    put = [
        pltpu.make_async_copy(held, dst, put_sem.at[n])
        for n, (_, held, dst) in enumerate(blocks)
        if dst is not None
    ]
    for one in fetch:
        one.start()
    fetch[0].wait()
    fetch[1].wait()
    slot = slot_v[...].T
    low, high = slot & 127, slot // 128
    total = jnp.zeros((TOK, PICKS), F32)
    for a in range(4):
        part = jnp.take_along_axis(pair_v[:, pl.ds(a * 128, 128)], low, axis=1)
        total = jnp.where(high == a, part, total)
    picked[...] = total.T
    last = pltpu.make_async_copy(picked, out_ref, put_sem.at[0])
    last.start()
    for one, two in zip(fetch[2:], put):
        one.wait()
        two.start()
    for one in put:
        one.wait()
    last.wait()


def shards(lookup_slot, lookup_weight, owner_route, values, out_grad):
    slot_t = lookup_slot.transpose(1, 2, 0).reshape(PICKS, TOK)
    weight_t = lookup_weight.transpose(1, 2, 0).reshape(PICKS, TOK)
    hbm = pl.BlockSpec(memory_space=pltpu.HBM)
    vmem, anywhere = pl.BlockSpec(memory_space=pltpu.VMEM), pl.BlockSpec(memory_space=pl.ANY)
    out, gv, pair = pl.pallas_call(
        exchange,
        out_shape=(
            jax.ShapeDtypeStruct((TOK, C * FEAT), BF16),
            jax.ShapeDtypeStruct((ROWS, FEAT), F32),
            jax.ShapeDtypeStruct((TOK, 2 * ROWS), F32),
        ),
        in_specs=[anywhere] * 5,
        out_specs=(anywhere, anywhere, anywhere),
        scratch_shapes=[
            pltpu.VMEM((Z, 2, HALF, FEAT), BF16),
            pltpu.VMEM((C, Y, TOK, FEAT), BF16),
            pltpu.VMEM((Y, MSG, ROWS), BF16),
            pltpu.VMEM((C, Y, MSG, ROWS), BF16),
            pltpu.VMEM((2, Y * SLOTS, TOK), BF16),
            pltpu.VMEM((2 * ROWS, TOK), BF16),
            pltpu.VMEM((PICKS, TOK), jnp.int32),
            pltpu.VMEM((PICKS, TOK), F32),
            pltpu.VMEM((2, TOK), jnp.int32),
            pltpu.VMEM((TOK, 2 * ROWS), F32),
            pltpu.VMEM((ROWS, FEAT), F32),
            pltpu.VMEM((16, ROWS, 2 * TOK), BF16),
            pltpu.VMEM((Z, 16 * 16, ROWS), BF16),
            pltpu.VMEM((Z, 16 * 16, FEAT), BF16),
            pltpu.VMEM((Z, 16 * 16, FEAT), BF16),
            pltpu.VMEM((K, X, Z, 32, ROWS), BF16),
            pltpu.VMEM((X, Z, 32, ROWS), BF16),
            pltpu.VMEM((X, Z, 32, ROWS), BF16),
            pltpu.VMEM((3, Z, 32, ROWS), BF16),
            pltpu.VMEM((4, Z, CAP, ROWS), F32),
            pltpu.VMEM((5, Y * SLOTS, ROWS), BF16),
            pltpu.VMEM((C, Y, TOK, FEAT), BF16),
            pltpu.VMEM((4, TOK, FEAT), BF16),
            pltpu.VMEM((4, TOK, FEAT), BF16),
            pltpu.VMEM((C, TOK, FEAT), BF16),
            pltpu.VMEM((C, TOK, FEAT), BF16),
            pltpu.VMEM((8, 2, 2, HALF, FEAT), BF16),
            pltpu.VMEM((8, 2, 2, HALF, FEAT), BF16),
            pltpu.SemaphoreType.DMA((SEMS,)),
            pltpu.SemaphoreType.DMA((SEMS,)),
            pltpu.SemaphoreType.DMA((8,)),
        ],
        compiler_params=pltpu.CompilerParams(
            collective_id=0, has_side_effects=True, vmem_limit_bytes=58 * 1024 * 1024
        ),
        name="exchange",
    )(slot_t, weight_t, owner_route.T, out_grad, values)
    grad_weight, out, gv = pl.pallas_call(
        pick,
        out_shape=(
            jax.ShapeDtypeStruct((PICKS, TOK), F32),
            jax.ShapeDtypeStruct(out.shape, out.dtype),
            jax.ShapeDtypeStruct(gv.shape, gv.dtype),
        ),
        in_specs=[hbm] * 4,
        out_specs=(hbm, hbm, hbm),
        scratch_shapes=[
            pltpu.VMEM((TOK, 2 * ROWS), F32),
            pltpu.VMEM((PICKS, TOK), jnp.int32),
            pltpu.VMEM((PICKS, TOK), F32),
            pltpu.VMEM((TOK, C * FEAT), BF16),
            pltpu.VMEM((ROWS, FEAT), F32),
            pltpu.SemaphoreType.DMA((14,)),
            pltpu.SemaphoreType.DMA((14,)),
        ],
        name="pick",
    )(pair, slot_t, out, gv)
    return out, gv, grad_weight.reshape(4, 32, TOK).transpose(2, 0, 1)


def solution(mesh):
    return jax.shard_map(
        shards,
        mesh=mesh,
        in_specs=(
            P(("dp", "mem"), None, None),
            P(("dp", "mem"), None, None),
            P(("dp", "mem"), None),
            P("mem", None),
            P(("dp", "mem"), None),
        ),
        out_specs=(P(("dp", "mem"), None), P("mem", "dp"), P(("dp", "mem"), None, None)),
        check_vma=False,
    )
```

profile of v0, /device:TPU:1, one launch (start us, length us, event | category | flops | bytes accessed | tf_op | source)
XLA Modules:
  0.0 111.8 jit_solution(14440300677767514941)
XLA Ops:
  0.6 108.5 %exchange.1 = (bf16[128,4096]{1,0:T(8,128)(2,1)}, f32[256,512]{1,0:T(8,128)}, f32[128,512]{1,0:T(8,128)}) custom-call(s32[128,128]{1,0:T(8,128)} %bitcast.10, f32[128,128]{1,0:T(8,128)} %bitcast.12, s32[2,128]{1,0:T(2,128)} %bitcast.13, bf16[128,4096]{1,0:T(8,128)(2,1)} %og.1, bf16[256,4096]{1,0:T(8,128)(2,1)} %values.1), custom_call_target="tpu_custom_call" | custom-call | tf_op jit(solution)/shard_map/exchange/pallas_call | solution.py:633
  109.1 2.7 %pick.1 = (f32[128,128]{1,0:T(8,128)}, bf16[128,4096]{1,0:T(8,128)(2,1)}, f32[256,512]{1,0:T(8,128)}) custom-call(f32[128,512]{1,0:T(8,128)} %get-tuple-element.9.pair_in, s32[128,128]{1,0:T(8,128)} %bitcast.11, bf16[128,4096]{1,0:T(8,128)(2,1)} %get-tuple-element.10.out_in, f32[256,512]{1,0:T(8,128)} %get-tuple-element.11.gv_in), custom_call_target="tpu_custom_call" | custom-call | tf_op jit(solution)/shard_map/pick/pallas_call | solution.py:680
where the time goes:
time: 112 us
  Pallas kernels  111 us (99%)
    pallas_call x1, Pallas kernels, shards(): pl.pallas_call(exchange, out_shape=(jax.ShapeDtypeStruct((TOK, C * FEAT),...  108 us
    pallas_call x1, Pallas kernels, shards(): pl.pallas_call(pick, out_shape=(jax.ShapeDtypeStruct((PICKS, TOK), F32),...  2.69 us

commit v1 on v0

--- a/solution.py
+++ b/solution.py
@@ -202,6 +202,7 @@
     dense(1)
     c_step(2)
     dense(2)
+    c_step(4)
     z_step(1, 1)
     dense(3)
 
@@ -241,7 +242,6 @@
     wa[c, y] = wm[y]
     w_piece(0)
 
-    c_step(4)
     c_step(3)
     z_step(2, 0)
     c_step(5)

time: 112 us -> 113 us (level)
  no operation moved by 1% of the time
where the time goes in v1:
time: 113 us
  Pallas kernels  112 us (99%)
    pallas_call x1, Pallas kernels, shards(): pl.pallas_call(exchange, out_shape=(jax.ShapeDtypeStruct((TOK, C * FEAT),...  109 us
    pallas_call x1, Pallas kernels, shards(): pl.pallas_call(pick, out_shape=(jax.ShapeDtypeStruct((PICKS, TOK), F32),...  2.69 us

profile of v1, /device:TPU:1, one launch (start us, length us, event | category | flops | bytes accessed | tf_op | source)
XLA Modules:
  0.0 112.5 jit_solution(2195164921053524653)
XLA Ops:
  0.6 109.2 %exchange.1 = (bf16[128,4096]{1,0:T(8,128)(2,1)}, f32[256,512]{1,0:T(8,128)}, f32[128,512]{1,0:T(8,128)}) custom-call(s32[128,128]{1,0:T(8,128)} %bitcast.10, f32[128,128]{1,0:T(8,128)} %bitcast.12, s32[2,128]{1,0:T(2,128)} %bitcast.13, bf16[128,4096]{1,0:T(8,128)(2,1)} %og.1, bf16[256,4096]{1,0:T(8,128)(2,1)} %values.1), custom_call_target="tpu_custom_call" | custom-call | tf_op jit(solution)/shard_map/exchange/pallas_call | solution.py:633
  109.8 2.7 %pick.1 = (f32[128,128]{1,0:T(8,128)}, bf16[128,4096]{1,0:T(8,128)(2,1)}, f32[256,512]{1,0:T(8,128)}) custom-call(f32[128,512]{1,0:T(8,128)} %get-tuple-element.9.pair_in, s32[128,128]{1,0:T(8,128)} %bitcast.11, bf16[128,4096]{1,0:T(8,128)(2,1)} %get-tuple-element.10.out_in, f32[256,512]{1,0:T(8,128)} %get-tuple-element.11.gv_in), custom_call_target="tpu_custom_call" | custom-call | tf_op jit(solution)/shard_map/pick/pallas_call | solution.py:680
